TPU v7x, 32 devices: a whole 2x2x4 slice. The times are simulated.
32 devices in a mesh: span: 4 (over y, x), stream: 8 (over z, core).
Axes of the slice: x: 2, y: 2, z: 4, core: 2. Of those that a mesh axis runs over, the one named last changes fastest.
Arguments:
- state: float32 [6, 64, 16384], P(None, None, ('span', 'stream')), may hold values from -6 to 6
- stiffness: float32 [16384], P(('span', 'stream')), may hold values from 0.3 to 6
- crossing: int32 [2, 4096], P(None, ('span', 'stream')), may hold values from 0 to 511, as said below
- contact_send: int32 [2, 4, 32768], P(None, None, ('span', 'stream')), may hold values from 0 to 32767
- contact_recv: int32 [2, 4, 32768], P(None, None, ('span', 'stream')), may hold values from 0 to 32767
- contact_fill: int32 [2, 4, 256], P(None, None, ('span', 'stream')), may hold values from 0 to 128, as said below
Outputs:
- final_state: float32 [6, 64, 16384], P(None, None, ('span', 'stream'))
Inputs may be any that keep to these rules, and one draw needn't show every extreme that they name: `crossing`: each slab's 2 * 64 entries of one step are distinct and include slots 0 and 511. `contact_fill`: in each run of 8 blocks the live blocks come first; all full except the last live one; some runs have every block live.
All inputs are finite; a program needn't handle non-finite values.
Results may differ from a plain program's by a relative error of at most 0.0001.
Values sent between devices are 32-bit elements; how exact they have to be, the bound alone decides.
A program may use at most 128 MiB of HBM per device.

v0:
```python
import functools
import math

import jax
import jax.numpy as jnp
import ml_dtypes
import numpy as np
from jax import lax
from jax.experimental import pallas as pl
from jax.experimental.pallas import tpu as pltpu
from jax.sharding import PartitionSpec as P

STEPS = 2
MESH = pl.DeviceIdType.MESH
F32 = jnp.float32
BF16 = jnp.bfloat16
LANES = 128
HALF_SLOTS = 256
SUB = 256


def cosine_tables(nodes):
    k = np.arange(nodes)[:, None]
    n = np.arange(nodes)[None, :]
    basis = np.sqrt(2.0 / nodes) * np.cos(np.pi * (n + 0.5) * k / nodes)
    basis[0] /= math.sqrt(2.0)

    def stacked(matrix):
        high = matrix.astype(ml_dtypes.bfloat16)
        low = (matrix - high.astype(np.float64)).astype(ml_dtypes.bfloat16)
        return np.concatenate([high, high, low, np.zeros_like(low)], axis=1)

    lam = 2.0 - 2.0 * np.cos(np.pi * np.arange(nodes) / nodes)
    lam = np.repeat(lam[:, None], LANES, axis=1).astype(np.float32)
    return stacked(basis), stacked(basis.T), lam


def split(x):
    high = x.astype(BF16)
    return high, (x - high.astype(F32)).astype(BF16)


def split3(x):
    high, rest = x.astype(BF16), None
    rest = x - high.astype(F32)
    mid = rest.astype(BF16)
    return high, mid, (rest - mid.astype(F32)).astype(BF16)


def dot(a, b):
    return jnp.dot(a, b, preferred_element_type=F32)


def dot_nt(a, b):
    return lax.dot_general(a, b, (((1,), (1,)), ((), ())), preferred_element_type=F32)


def along_nodes(matrix, block):
    high, low = split(block)
    return dot(matrix, jnp.concatenate([high, low, high], axis=0))


def tall(row, rows):
    tile = jnp.broadcast_to(row, (16, row.shape[1])).astype(BF16)
    return jnp.concatenate([tile] * (rows // 16), axis=0)


def kernel(
    groups, n_stream,
    state_hbm, coef_hbm, crossing_hbm, csend_hbm, crecv_hbm, cfill_hbm, mats_hbm, lam_hbm,
    out,
    state, coef0, crossing, csend, crecv, cfill, mats, lam, iota,
    xh, parts, hot, local, acc, scale, base, ahead, cross_col, moving, coef_in, coef_out, sbuf, rbuf, mout, min_,
    l_sem, c_send, c_recv, p_send, p_recv, m_send, m_recv,
):
    fields, nodes, fdev = state.shape
    quota = csend.shape[2]
    cross = crossing.shape[1]
    half = cross // 2
    npos = 3 * nodes
    i = lax.axis_index("span")
    j = lax.axis_index("stream")
    down_dev = (i, lax.rem(j + 1, n_stream))
    up_dev = (i, lax.rem(j + n_stream - 1, n_stream))
    pos_at, rot_at = slice(0, npos), slice(npos, 2 * npos)

    def mod(v):
        return lax.rem(v, groups)

    barrier = pltpu.get_barrier_semaphore()
    for dev in (down_dev, up_dev):
        pl.semaphore_signal(barrier, inc=1, device_id=dev, device_id_type=MESH)
    for k in range(1, groups):
        pl.semaphore_signal(
            barrier, inc=1, device_id=(mod(i + k), j), device_id_type=MESH
        )

    moves = [
        (state_hbm.at[0:3], state.at[0:3]),
        (csend_hbm, csend),
        (cfill_hbm, cfill),
        (crecv_hbm, crecv),
        (crossing_hbm, crossing),
        (coef_hbm, coef0),
        (mats_hbm, mats),
        (lam_hbm, lam),
        (state_hbm.at[3:6], state.at[3:6]),
    ]
    loads = [
        pltpu.make_async_copy(src, dst, l_sem.at[n])
        for n, (src, dst) in enumerate(moves)
    ]
    for copy in loads:
        copy.start()

    iota[...] = (
        lax.broadcasted_iota(jnp.int32, (HALF_SLOTS, LANES), 0).astype(F32).astype(BF16)
    )
    lane = lax.broadcasted_iota(jnp.int32, (1, LANES), 1)
    node_iota = lax.broadcasted_iota(jnp.int32, (nodes, SUB), 0)

    def slot_hot(slot, q):
        pieces = []
        for part in range(fdev // HALF_SLOTS):
            rel = slot - part * HALF_SLOTS
            inside = (rel >= 0) & (rel < HALF_SLOTS)
            val = jnp.where(inside, rel, -1).astype(F32)
            wide = jnp.concatenate([iota[...]] * (q // LANES), axis=1)
            same = wide == tall(val, HALF_SLOTS)
            pieces.append(jnp.where(same, BF16(1), BF16(0)))
        return jnp.concatenate(pieces, axis=0)

    def locate(index):
        if fdev & (fdev - 1) == 0:
            return index & (fdev - 1), index >> (fdev.bit_length() - 1)
        return lax.rem(index, fdev), lax.div(index, fdev)

    def gather(index, keep_at=None, sub=0):
        slot, node = locate(index)
        table = slot_hot(slot, SUB)
        if keep_at is not None:
            hot[keep_at, :, sub * SUB : (sub + 1) * SUB] = table
        picked = dot(parts[...], table)
        return at_nodes(picked[:npos] + picked[npos:], node)

    def at_nodes(picked, node):
        mask = node_iota == node
        return [
            jnp.sum(
                jnp.where(mask, picked[c * nodes : (c + 1) * nodes], 0.0),
                axis=0, keepdims=True,
            )
            for c in range(3)
        ]

    def set_parts(block):
        high, low = split(block)
        parts[:npos, :] = high
        parts[npos:, :] = low

    def forward(block):
        return along_nodes(mats[:nodes, : 3 * nodes].astype(BF16), block)

    def backward(block):
        back = mats[nodes:, : 3 * nodes].astype(BF16)
        return jnp.concatenate(
            [along_nodes(back, block[c * nodes : (c + 1) * nodes]) for c in range(3)],
            axis=0,
        )

    def set_scale(c):
        for b in range(fdev // LANES):
            at = slice(b * LANES, (b + 1) * LANES)
            scale[:, at] = 1.0 / (1.0 + lam[...] * c[:, at])

    def pair_copy(step, k):
        to = mod(i + 1 + k)
        return pltpu.make_async_remote_copy(
            src_ref=sbuf.at[step, to], dst_ref=rbuf.at[step, i],
            send_sem=p_send.at[step, to], recv_sem=p_recv.at[step, i],
            device_id=(to, j), device_id_type=MESH,
        )

    def pair_arrival(step, source):
        return pltpu.make_async_remote_copy(
            src_ref=sbuf.at[step, source], dst_ref=rbuf.at[step, source],
            send_sem=p_send.at[step, source], recv_sem=p_recv.at[step, source],
            device_id=(source, j), device_id_type=MESH,
        )

    first = lax.broadcasted_iota(jnp.int32, (npos // 2, cross), 1) < half

    def fibre_copies(step, h):
        return [
            pltpu.make_async_remote_copy(
                src_ref=mout.at[step, h, d], dst_ref=min_.at[step, h, d],
                send_sem=m_send.at[step, h, d], recv_sem=m_recv.at[step, h, d],
                device_id=dev, device_id_type=MESH,
            )
            for d, dev in enumerate((down_dev, up_dev))
        ]

    def leave(step, h, block, table):
        high, low = split(block)
        picked = dot(high, table) + dot(low, table)
        top, bottom = picked[: npos // 2], picked[npos // 2 :]
        mout[step, h, 0] = jnp.where(first, top, pltpu.roll(bottom, half, 1))
        mout[step, h, 1] = jnp.where(first, pltpu.roll(top, half, 1), bottom)
        for copy in fibre_copies(step, h):
            copy.start()

    def arrive(step, h):
        for copy in fibre_copies(step, h):
            copy.wait()
        above, below = min_[step, h, 0], min_[step, h, 1]
        return jnp.concatenate(
            [
                jnp.where(first, above, pltpu.roll(below, half, 1)),
                jnp.where(first, pltpu.roll(above, half, 1), below),
            ],
            axis=0,
        )

    def inserted(came, table):
        high, low = split(came)
        return dot_nt(high, table) + dot_nt(low, table)

    def send_gather(step, g, buf):
        fill = cfill[step, pl.ds(g, 1), :]
        for sub in range(quota // SUB):
            at = slice(sub * SUB, (sub + 1) * SUB)
            got = gather(csend[step, pl.ds(g, 1), at])
            for c in range(3):
                buf[c : c + 1, at] = got[c]
        for b in range(quota // LANES):
            live = lane < fill[:, b : b + 1]
            buf[3:4, b * LANES : (b + 1) * LANES] = jnp.where(live, 1.0, 0.0)

    def arrived_gather(step, g, moving, buf):
        for sub in range(quota // SUB):
            at = slice(sub * SUB, (sub + 1) * SUB)
            slot, node = locate(csend[step, pl.ds(g, 1), at])
            wide = jnp.concatenate([cross_col[...]] * (SUB // LANES), axis=1)
            table = jnp.where(wide == slot, 1.0, 0.0).astype(BF16)
            got = at_nodes(dot(moving, jnp.concatenate([table, table], axis=0)), node)
            for c in range(3):
                buf[c : c + 1, at] = ahead[g, c : c + 1, at] + got[c]
        buf[3:4, :] = ahead[g, 3:4, :]

    for copy in loads[:3]:
        copy.wait()
    set_parts(jnp.concatenate([state[c] for c in range(3)], axis=0))

    for step in range(STEPS):
        if step == 0:
            send_gather(step, i, rbuf.at[step, i])
            pl.semaphore_wait(barrier, groups + 1)

            @pl.loop(0, groups - 1)
            def _(k):
                to = mod(i + 1 + k)
                send_gather(step, to, sbuf.at[step, to])
                pair_copy(step, k).start()

        else:

            @pl.loop(0, groups - 1)
            def _(k):
                to = mod(i + 1 + k)
                arrived_gather(step, to, moving[...], sbuf.at[step, to])
                pair_copy(step, k).start()

            arrived_gather(step, i, moving[...], rbuf.at[step, i])
            set_parts(base[...] + inserted(came_nodes, cross_hot[step - 1]))

        if step == 0:
            for copy in loads[3:]:
                copy.wait()
            cross_hot = [slot_hot(crossing[s : s + 1, :], cross) for s in range(STEPS)]
            ones = jnp.ones((16, cross), BF16)
            keeps = [1.0 - dot_nt(ones, t)[:1] for t in cross_hot]
            coef = coef0[...]
            wide_coef = jnp.broadcast_to(coef, (16, fdev))
            leaving = sum(dot(p, cross_hot[0]) for p in split3(wide_coef))
            coef_out[...] = leaving[:8]
            coef_copies = [
                pltpu.make_async_remote_copy(
                    src_ref=coef_out, dst_ref=coef_in.at[d],
                    send_sem=c_send.at[d], recv_sem=c_recv.at[d],
                    device_id=dev, device_id_type=MESH,
                )
                for d, dev in enumerate((down_dev, up_dev))
            ]
            for copy in coef_copies:
                copy.start()
            set_scale(coef)
            for c in range(3, fields):
                xh[c * nodes : (c + 1) * nodes, :] = forward(state[c]) * scale[...]
            leave(step, 1, xh[rot_at, :], cross_hot[step])

        @pl.loop(0, groups)
        def _(g):
            for sub in range(quota // SUB):
                at = slice(sub * SUB, (sub + 1) * SUB)
                got = gather(crecv[step, pl.ds(g, 1), at], g, sub)
                for c in range(3):
                    local[g, c : c + 1, at] = got[c]

        if step == 0:
            for c in range(3):
                xh[c * nodes : (c + 1) * nodes, :] = forward(state[c])
        else:
            for copy in coef_copies:
                copy.wait()
            arrived = jnp.where(
                lax.broadcasted_iota(jnp.int32, (8, cross), 1) < half,
                coef_in[0], coef_in[1],
            )
            arrived = jnp.concatenate([arrived, arrived], axis=0)
            moved = sum(dot_nt(p, cross_hot[0]) for p in split3(arrived))
            set_scale(coef * keeps[0] + moved[:1])
            xh[pos_at, :] = xh[pos_at, :] * keeps[0] + inserted(came, cross_hot[0])
            turned = inserted(arrive(0, 1), cross_hot[0])
            for c in range(3):
                at = slice(npos + c * nodes, npos + (c + 1) * nodes)
                moved_in = turned[c * nodes : (c + 1) * nodes]
                xh[at, :] = (xh[at, :] * keeps[0] + moved_in) * scale[...]
            leave(step, 1, xh[rot_at, :], cross_hot[step])

        acc[...] = jnp.zeros_like(acc)

        def scatter(g):
            delta = rbuf[step, g, 0:3] - local[g, 0:3]
            radius = jnp.sum(delta * delta, axis=0, keepdims=True)
            live = rbuf[step, g, 3:4] > 0.5
            force = jnp.where(live, 0.5 * delta / (1.0 + radius), 0.0)
            node = locate(crecv[step, pl.ds(g, 1), :])[1].astype(F32)
            wide = jnp.concatenate([iota[:nodes]] * (quota // LANES), axis=1)
            node_hot = jnp.where(wide == tall(node, nodes), BF16(1), BF16(0))
            high, low = split(force)
            spread = [
                node_hot * tall(p[c : c + 1].astype(F32), nodes)
                for p in (high, low)
                for c in range(3)
            ]
            acc[...] += dot_nt(jnp.concatenate(spread, axis=0), hot[g])

        scatter(i)

        @pl.loop(0, groups - 1)
        def _(k):
            source = mod(i + groups - 1 - k)
            pair_arrival(step, source).wait_recv()
            scatter(source)

        for c in range(3):
            at = slice(c * nodes, (c + 1) * nodes)
            low_at = slice(npos + c * nodes, npos + (c + 1) * nodes)
            push = forward(acc[at, :] + acc[low_at, :])
            xh[at, :] = (xh[at, :] + push) * scale[...]
        table, keep = cross_hot[step], keeps[step]
        leave(step, 0, xh[pos_at, :], table)

        base[...] = backward(xh[pos_at, :] * keep)
        if step < STEPS - 1:
            set_parts(base[...])
            column = jnp.broadcast_to(crossing[step : step + 1, :].astype(F32), (LANES, cross))
            cross_col[...] = column.T.astype(jnp.int32)

            @pl.loop(0, groups)
            def _(g):
                send_gather(step + 1, g, ahead.at[g])

            came = arrive(step, 0)
            came_nodes = backward(came)
            moving[...] = jnp.concatenate(split(came_nodes), axis=1)
        else:
            turned = backward(xh[rot_at, :] * keep)
            turned += inserted(backward(arrive(step, 1)), table)
            for c in range(3):
                out[3 + c] = turned[c * nodes : (c + 1) * nodes]
            placed = base[...] + inserted(backward(arrive(step, 0)), table)
            for c in range(3):
                out[c] = placed[c * nodes : (c + 1) * nodes]

    for step in range(STEPS):

        @pl.loop(0, groups - 1)
        def _(k):
            pair_copy(step, k).wait_send()


def per_device(groups, n_stream, state, stiffness, crossing, csend, crecv, cfill):
    fields, nodes, fdev = state.shape
    quota = csend.shape[2]
    cross = crossing.shape[1]
    rows = fields * nodes
    fwd, inv, lam = cosine_tables(nodes)
    mats = np.concatenate([fwd, inv], axis=0).astype(np.float32)
    hbm = pl.BlockSpec(memory_space=pltpu.HBM)
    return pl.pallas_call(
        functools.partial(kernel, groups, n_stream),
        out_shape=pltpu.VMEM(state.shape, F32),
        in_specs=[hbm] * 8,
        out_specs=pl.BlockSpec(memory_space=pltpu.VMEM),
        scratch_shapes=[
            pltpu.VMEM(state.shape, F32),
            pltpu.VMEM((1, fdev), F32),
            pltpu.VMEM(crossing.shape, jnp.int32),
            pltpu.VMEM(csend.shape, jnp.int32),
            pltpu.VMEM(crecv.shape, jnp.int32),
            pltpu.VMEM(cfill.shape, jnp.int32),
            pltpu.VMEM(mats.shape, F32),
            pltpu.VMEM(lam.shape, F32),
            pltpu.VMEM((HALF_SLOTS, LANES), BF16),
            pltpu.VMEM((rows, fdev), F32),
            pltpu.VMEM((6 * nodes, fdev), BF16),
            pltpu.VMEM((groups, fdev, quota), BF16),
            pltpu.VMEM((groups, 4, quota), F32),
            pltpu.VMEM((6 * nodes, fdev), F32),
            pltpu.VMEM((nodes, fdev), F32),
            pltpu.VMEM((3 * nodes, fdev), F32),
            pltpu.VMEM((groups, 4, quota), F32),
            pltpu.VMEM((cross, LANES), jnp.int32),
            pltpu.VMEM((3 * nodes, 2 * cross), BF16),
            pltpu.VMEM((2, 8, cross), F32),
            pltpu.VMEM((8, cross), F32),
            pltpu.VMEM((STEPS, groups, 4, quota), F32),
            pltpu.VMEM((STEPS, groups, 4, quota), F32),
            pltpu.VMEM((STEPS, 2, 2, rows // 4, cross), F32),
            pltpu.VMEM((STEPS, 2, 2, rows // 4, cross), F32),
            pltpu.SemaphoreType.DMA((9,)),
            pltpu.SemaphoreType.DMA((2,)),
            pltpu.SemaphoreType.DMA((2,)),
            pltpu.SemaphoreType.DMA((STEPS, groups)),
            pltpu.SemaphoreType.DMA((STEPS, groups)),
            pltpu.SemaphoreType.DMA((STEPS, 2, 2)),
            pltpu.SemaphoreType.DMA((STEPS, 2, 2)),
        ],
        compiler_params=pltpu.CompilerParams(
            collective_id=0, has_side_effects=True, vmem_limit_bytes=40 * 2**20
        ),
    )(
        *(
            pltpu.with_memory_space_constraint(x, pltpu.HBM)
            for x in (
                state, stiffness.reshape(1, fdev), crossing, csend, crecv, cfill,
                jnp.asarray(mats), jnp.asarray(lam),
            )
        )
    )


def solution(mesh):
    cells = ("span", "stream")
    placed = (
        P(None, None, cells),
        P(cells),
        P(None, cells),
        P(None, None, cells),
        P(None, None, cells),
        P(None, None, cells),
    )
    return jax.shard_map(
        functools.partial(per_device, mesh.shape["span"], mesh.shape["stream"]),
        mesh=mesh,
        in_specs=placed,
        out_specs=P(None, None, cells),
        check_vma=False,
    )
```

profile of v0, /device:TPU:0, one launch (start us, length us, event | category | flops | bytes accessed | tf_op | source)
XLA Modules:
  0.0 29.4 jit_solution(8858086636907473448)
XLA Ops:
  0.0 28.5 %shard_map.82 = f32[6,64,512]{2,1,0:T(8,128)S(1)} custom-call(f32[6,64,512]{2,1,0:T(8,128)} %state_hbm.1, f32[1,512]{1,0:T(1,128)} %bitcast.1, s32[2,128]{1,0:T(2,128)} %crossing_hbm.1, s32[2,4,1024]{2,1,0:T(4,128)} %csend_hbm.1, s32[2,4,1024]{2,1,0:T(4,128)} %crecv_hbm.1, s32[2,4,8]{2,1,0:T(4,128)} %cfill_hbm.1, f32[128,256]{1,0:T(8,128)} %constant.4.clone.mats_hbm, ...), custom_call_target="tpu_custom_call" | custom-call | tf_op jit(solution)/shard_map/pallas_call | solution.py:401
  28.5 0.9 %copy.10 = f32[6,64,512]{2,1,0:T(8,128)} copy(f32[6,64,512]{2,1,0:T(8,128)S(1)} %shard_map.82) | data formatting | bytes 1572864
where the time goes:
time: 29.5 us; the launch traced here: 29.4 us
  Pallas kernels  28.5 us (97%)
  local copies, waits for them, and re-layouts  0.88 us (3%)
    pallas_call x1, Pallas kernels, per_device(): pl.pallas_call(functools.partial(kernel, groups, n_stream), out_shape=plt...  28.5 us
    unnamed x1, local copies, waits for them, and re-layouts  0.88 us

commit v1 on v0

--- a/solution.py
+++ b/solution.py
@@ -16,7 +16,7 @@
 BF16 = jnp.bfloat16
 LANES = 128
 HALF_SLOTS = 256
-SUB = 256
+SUB = 512
 
 
 def cosine_tables(nodes):

time: 29.5 us -> 29.5 us (level)
  no operation moved by 1% of the time
where the time goes in v1:
time: 29.5 us; the launch traced here: 29.3 us
  Pallas kernels  28.4 us (96%)
  local copies, waits for them, and re-layouts  0.88 us (3%)
    pallas_call x1, Pallas kernels, per_device(): pl.pallas_call(functools.partial(kernel, groups, n_stream), out_shape=plt...  28.4 us
    unnamed x1, local copies, waits for them, and re-layouts  0.88 us

profile of v1, /device:TPU:0, one launch (start us, length us, event | category | flops | bytes accessed | tf_op | source)
XLA Modules:
  0.0 29.3 jit_solution(4930289713623069965)
XLA Ops:
  0.0 28.4 %shard_map.82 = f32[6,64,512]{2,1,0:T(8,128)S(1)} custom-call(f32[6,64,512]{2,1,0:T(8,128)} %state_hbm.1, f32[1,512]{1,0:T(1,128)} %bitcast.1, s32[2,128]{1,0:T(2,128)} %crossing_hbm.1, s32[2,4,1024]{2,1,0:T(4,128)} %csend_hbm.1, s32[2,4,1024]{2,1,0:T(4,128)} %crecv_hbm.1, s32[2,4,8]{2,1,0:T(4,128)} %cfill_hbm.1, f32[128,256]{1,0:T(8,128)} %constant.4.clone.mats_hbm, ...), custom_call_target="tpu_custom_call" | custom-call | tf_op jit(solution)/shard_map/pallas_call | solution.py:401
  28.5 0.9 %copy.10 = f32[6,64,512]{2,1,0:T(8,128)} copy(f32[6,64,512]{2,1,0:T(8,128)S(1)} %shard_map.82) | data formatting | bytes 1572864

commit v2 on v0

--- a/solution.py
+++ b/solution.py
@@ -17,6 +17,7 @@
 LANES = 128
 HALF_SLOTS = 256
 SUB = 256
+BY_LANES = 2
 
 
 def cosine_tables(nodes):
@@ -70,7 +71,7 @@
     state_hbm, coef_hbm, crossing_hbm, csend_hbm, crecv_hbm, cfill_hbm, mats_hbm, lam_hbm,
     out,
     state, coef0, crossing, csend, crecv, cfill, mats, lam, iota,
-    xh, parts, hot, local, acc, scale, base, ahead, cross_col, moving, coef_in, coef_out, sbuf, rbuf, mout, min_,
+    xh, parts, exact, hot, local, acc, scale, base, ahead, cross_col, moving, coef_in, coef_out, sbuf, rbuf, mout, min_,
     l_sem, c_send, c_recv, p_send, p_recv, m_send, m_recv,
 ):
     fields, nodes, fdev = state.shape
@@ -143,8 +144,40 @@
         picked = dot(parts[...], table)
         return at_nodes(picked[:npos] + picked[npos:], node)
 
+    def lane_gather(index):
+        slot, node = locate(index)
+        at_lane = jnp.broadcast_to(slot & (LANES - 1), (npos, LANES))
+        block = jnp.broadcast_to(slot >> 7, (npos, LANES))
+        picked = jnp.zeros((npos, LANES), F32)
+        for b in range(fdev // LANES):
+            part = jnp.take_along_axis(
+                exact[:, b * LANES : (b + 1) * LANES], at_lane, axis=1,
+                mode="promise_in_bounds",
+            )
+            picked = jnp.where(block == b, part, picked)
+        return at_nodes(picked, node)
+
+    def gather_group(indices, step, g, buf, keep_at=None):
+        subs = quota // SUB
+        for sub in range(subs):
+            at = slice(sub * SUB, (sub + 1) * SUB)
+            index = indices[step, pl.ds(g, 1), at]
+            if sub < subs - BY_LANES:
+                got = gather(index, keep_at, sub)
+                for c in range(3):
+                    buf[c : c + 1, at] = got[c]
+                continue
+            if keep_at is not None:
+                hot[keep_at, :, at] = slot_hot(locate(index)[0], SUB)
+            for n in range(SUB // LANES):
+                piece = slice(n * LANES, (n + 1) * LANES)
+                to = slice(sub * SUB + n * LANES, sub * SUB + (n + 1) * LANES)
+                got = lane_gather(index[:, piece])
+                for c in range(3):
+                    buf[c : c + 1, to] = got[c]
+
     def at_nodes(picked, node):
-        mask = node_iota == node
+        mask = node_iota[:, : node.shape[1]] == node
         return [
             jnp.sum(
                 jnp.where(mask, picked[c * nodes : (c + 1) * nodes], 0.0),
@@ -157,6 +190,7 @@
         high, low = split(block)
         parts[:npos, :] = high
         parts[npos:, :] = low
+        exact[...] = block
 
     def forward(block):
         return along_nodes(mats[:nodes, : 3 * nodes].astype(BF16), block)
@@ -227,11 +261,7 @@
 
     def send_gather(step, g, buf):
         fill = cfill[step, pl.ds(g, 1), :]
-        for sub in range(quota // SUB):
-            at = slice(sub * SUB, (sub + 1) * SUB)
-            got = gather(csend[step, pl.ds(g, 1), at])
-            for c in range(3):
-                buf[c : c + 1, at] = got[c]
+        gather_group(csend, step, g, buf)
         for b in range(quota // LANES):
             live = lane < fill[:, b : b + 1]
             buf[3:4, b * LANES : (b + 1) * LANES] = jnp.where(live, 1.0, 0.0)
@@ -300,11 +330,7 @@
 
         @pl.loop(0, groups)
         def _(g):
-            for sub in range(quota // SUB):
-                at = slice(sub * SUB, (sub + 1) * SUB)
-                got = gather(crecv[step, pl.ds(g, 1), at], g, sub)
-                for c in range(3):
-                    local[g, c : c + 1, at] = got[c]
+            gather_group(crecv, step, g, local.at[g], g)
 
         if step == 0:
             for c in range(3):
@@ -415,6 +441,7 @@
             pltpu.VMEM((HALF_SLOTS, LANES), BF16),
             pltpu.VMEM((rows, fdev), F32),
             pltpu.VMEM((6 * nodes, fdev), BF16),
+            pltpu.VMEM((3 * nodes, fdev), F32),
             pltpu.VMEM((groups, fdev, quota), BF16),
             pltpu.VMEM((groups, 4, quota), F32),
             pltpu.VMEM((6 * nodes, fdev), F32),

time: 29.5 us -> 29.5 us (level)
  no operation moved by 1% of the time
where the time goes in v2:
time: 29.5 us; the launch traced here: 29.4 us
  Pallas kernels  28.5 us (97%)
  local copies, waits for them, and re-layouts  0.88 us (3%)
    pallas_call x1, Pallas kernels, per_device(): pl.pallas_call(functools.partial(kernel, groups, n_stream), out_shape=plt...  28.5 us
    unnamed x1, local copies, waits for them, and re-layouts  0.88 us

profile of v2, /device:TPU:0, one launch (start us, length us, event | category | flops | bytes accessed | tf_op | source)
XLA Modules:
  0.0 29.4 jit_solution(16476348055129679934)
XLA Ops:
  0.0 28.5 %shard_map.82 = f32[6,64,512]{2,1,0:T(8,128)S(1)} custom-call(f32[6,64,512]{2,1,0:T(8,128)} %state_hbm.1, f32[1,512]{1,0:T(1,128)} %bitcast.1, s32[2,128]{1,0:T(2,128)} %crossing_hbm.1, s32[2,4,1024]{2,1,0:T(4,128)} %csend_hbm.1, s32[2,4,1024]{2,1,0:T(4,128)} %crecv_hbm.1, s32[2,4,8]{2,1,0:T(4,128)} %cfill_hbm.1, f32[128,256]{1,0:T(8,128)} %constant.4.clone.mats_hbm, ...), custom_call_target="tpu_custom_call" | custom-call | tf_op jit(solution)/shard_map/pallas_call | solution.py:427
  28.5 0.9 %copy.10 = f32[6,64,512]{2,1,0:T(8,128)} copy(f32[6,64,512]{2,1,0:T(8,128)S(1)} %shard_map.82) | data formatting | bytes 1572864

commit v3 on v0

--- a/solution.py
+++ b/solution.py
@@ -70,7 +70,7 @@
     state_hbm, coef_hbm, crossing_hbm, csend_hbm, crecv_hbm, cfill_hbm, mats_hbm, lam_hbm,
     out,
     state, coef0, crossing, csend, crecv, cfill, mats, lam, iota,
-    xh, parts, hot, local, acc, scale, base, ahead, cross_col, moving, coef_in, coef_out, sbuf, rbuf, mout, min_,
+    xh, parts, hot, local, acc, scale, base, ahead, cross_col, moving, hotx, spreads, lead, accx, coef_in, coef_out, sbuf, rbuf, mout, min_,
     l_sem, c_send, c_recv, p_send, p_recv, m_send, m_recv,
 ):
     fields, nodes, fdev = state.shape
@@ -201,8 +201,13 @@
         ]
 
     def leave(step, h, block, table):
+        send_off(step, h, pick(block, table))
+
+    def pick(block, table):
         high, low = split(block)
-        picked = dot(high, table) + dot(low, table)
+        return dot(high, table) + dot(low, table)
+
+    def send_off(step, h, picked):
         top, bottom = picked[: npos // 2], picked[npos // 2 :]
         mout[step, h, 0] = jnp.where(first, top, pltpu.roll(bottom, half, 1))
         mout[step, h, 1] = jnp.where(first, pltpu.roll(top, half, 1), bottom)
@@ -298,11 +303,18 @@
                 xh[c * nodes : (c + 1) * nodes, :] = forward(state[c]) * scale[...]
             leave(step, 1, xh[rot_at, :], cross_hot[step])
 
+        column = jnp.broadcast_to(crossing[step : step + 1, :].astype(F32), (LANES, cross))
+        cross_col[...] = column.T.astype(jnp.int32)
+
         @pl.loop(0, groups)
         def _(g):
             for sub in range(quota // SUB):
                 at = slice(sub * SUB, (sub + 1) * SUB)
-                got = gather(crecv[step, pl.ds(g, 1), at], g, sub)
+                index = crecv[step, pl.ds(g, 1), at]
+                wide = jnp.concatenate([cross_col[...]] * (SUB // LANES), axis=1)
+                same = wide == locate(index)[0]
+                hotx[g, :, at] = jnp.where(same, 1.0, 0.0).astype(BF16)
+                got = gather(index, g, sub)
                 for c in range(3):
                     local[g, c : c + 1, at] = got[c]
 
@@ -318,7 +330,10 @@
             )
             arrived = jnp.concatenate([arrived, arrived], axis=0)
             moved = sum(dot_nt(p, cross_hot[0]) for p in split3(arrived))
-            set_scale(coef * keeps[0] + moved[:1])
+            coef = coef * keeps[0] + moved[:1]
+            wide_coef = jnp.broadcast_to(coef, (16, fdev))
+            leaving = sum(dot(p, cross_hot[step]) for p in split3(wide_coef))
+            set_scale(coef)
             xh[pos_at, :] = xh[pos_at, :] * keeps[0] + inserted(came, cross_hot[0])
             turned = inserted(arrive(0, 1), cross_hot[0])
             for c in range(3):
@@ -327,7 +342,9 @@
                 xh[at, :] = (xh[at, :] * keeps[0] + moved_in) * scale[...]
             leave(step, 1, xh[rot_at, :], cross_hot[step])
 
-        acc[...] = jnp.zeros_like(acc)
+        lead[...] = pick(xh[pos_at, :], cross_hot[step])
+        scale_x = 1.0 / (1.0 + lam[...] * leaving[:1])
+        accx[...] = jnp.zeros_like(accx)
 
         def scatter(g):
             delta = rbuf[step, g, 0:3] - local[g, 0:3]
@@ -343,7 +360,9 @@
                 for p in (high, low)
                 for c in range(3)
             ]
-            acc[...] += dot_nt(jnp.concatenate(spread, axis=0), hot[g])
+            spread = jnp.concatenate(spread, axis=0)
+            spreads[g] = spread
+            accx[...] += dot_nt(spread, hotx[g])
 
         scatter(i)
 
@@ -353,19 +372,31 @@
             pair_arrival(step, source).wait_recv()
             scatter(source)
 
-        for c in range(3):
+        def pushed(total, c):
             at = slice(c * nodes, (c + 1) * nodes)
             low_at = slice(npos + c * nodes, npos + (c + 1) * nodes)
-            push = forward(acc[at, :] + acc[low_at, :])
+            return at, forward(total[at, :] + total[low_at, :])
+
+        leavers = []
+        for c in range(3):
+            at, push = pushed(accx, c)
+            leavers.append((lead[at, :] + push) * scale_x)
+        send_off(step, 0, jnp.concatenate(leavers, axis=0))
+
+        acc[...] = jnp.zeros_like(acc)
+
+        @pl.loop(0, groups)
+        def _(g):
+            acc[...] += dot_nt(spreads[g], hot[g])
+
+        for c in range(3):
+            at, push = pushed(acc, c)
             xh[at, :] = (xh[at, :] + push) * scale[...]
         table, keep = cross_hot[step], keeps[step]
-        leave(step, 0, xh[pos_at, :], table)
 
         base[...] = backward(xh[pos_at, :] * keep)
         if step < STEPS - 1:
             set_parts(base[...])
-            column = jnp.broadcast_to(crossing[step : step + 1, :].astype(F32), (LANES, cross))
-            cross_col[...] = column.T.astype(jnp.int32)
 
             @pl.loop(0, groups)
             def _(g):
@@ -423,6 +454,10 @@
             pltpu.VMEM((groups, 4, quota), F32),
             pltpu.VMEM((cross, LANES), jnp.int32),
             pltpu.VMEM((3 * nodes, 2 * cross), BF16),
+            pltpu.VMEM((groups, cross, quota), BF16),
+            pltpu.VMEM((groups, 6 * nodes, quota), BF16),
+            pltpu.VMEM((3 * nodes, cross), F32),
+            pltpu.VMEM((6 * nodes, cross), F32),
             pltpu.VMEM((2, 8, cross), F32),
             pltpu.VMEM((8, cross), F32),
             pltpu.VMEM((STEPS, groups, 4, quota), F32),

time: 29.5 us -> 30.1 us (1.020)
  Pallas kernels: 28.5 us -> 29 us
    pallas_call x1, Pallas kernels: 28.5 us -> 29 us  [per_device(): pl.pallas_call(functools.partial(kernel, groups, n_stream), out_shape=plt...]
where the time goes in v3:
time: 30.1 us; the launch traced here: 29.9 us
  Pallas kernels  29 us (96%)
  local copies, waits for them, and re-layouts  0.88 us (3%)
    pallas_call x1, Pallas kernels, per_device(): pl.pallas_call(functools.partial(kernel, groups, n_stream), out_shape=plt...  29 us
    unnamed x1, local copies, waits for them, and re-layouts  0.88 us

profile of v3, /device:TPU:0, one launch (start us, length us, event | category | flops | bytes accessed | tf_op | source)
XLA Modules:
  0.0 29.9 jit_solution(10195276665171668063)
XLA Ops:
  0.0 29.0 %shard_map.82 = f32[6,64,512]{2,1,0:T(8,128)S(1)} custom-call(f32[6,64,512]{2,1,0:T(8,128)} %state_hbm.1, f32[1,512]{1,0:T(1,128)} %bitcast.1, s32[2,128]{1,0:T(2,128)} %crossing_hbm.1, s32[2,4,1024]{2,1,0:T(4,128)} %csend_hbm.1, s32[2,4,1024]{2,1,0:T(4,128)} %crecv_hbm.1, s32[2,4,8]{2,1,0:T(4,128)} %cfill_hbm.1, f32[128,256]{1,0:T(8,128)} %constant.4.clone.mats_hbm, ...), custom_call_target="tpu_custom_call" | custom-call | tf_op jit(solution)/shard_map/pallas_call | solution.py:432
  29.0 0.9 %copy.10 = f32[6,64,512]{2,1,0:T(8,128)} copy(f32[6,64,512]{2,1,0:T(8,128)S(1)} %shard_map.82) | data formatting | bytes 1572864

commit v4 on v2

--- a/solution.py
+++ b/solution.py
@@ -17,7 +17,7 @@
 LANES = 128
 HALF_SLOTS = 256
 SUB = 256
-BY_LANES = 2
+BY_LANES = 1
 
 
 def cosine_tables(nodes):

time: 29.5 us -> 29.1 us (0.986)
  Pallas kernels: 28.5 us -> 28 us
    pallas_call x1, Pallas kernels: 28.5 us -> 28 us  [per_device(): pl.pallas_call(functools.partial(kernel, groups, n_stream), out_shape=plt...]
where the time goes in v4:
time: 29.1 us; the launch traced here: 28.9 us
  Pallas kernels  28 us (96%)
  local copies, waits for them, and re-layouts  0.88 us (3%)
    pallas_call x1, Pallas kernels, per_device(): pl.pallas_call(functools.partial(kernel, groups, n_stream), out_shape=plt...  28 us
    unnamed x1, local copies, waits for them, and re-layouts  0.88 us

profile of v4, /device:TPU:0, one launch (start us, length us, event | category | flops | bytes accessed | tf_op | source)
XLA Modules:
  0.0 28.9 jit_solution(7790838310361705289)
XLA Ops:
  0.0 28.0 %shard_map.82 = f32[6,64,512]{2,1,0:T(8,128)S(1)} custom-call(f32[6,64,512]{2,1,0:T(8,128)} %state_hbm.1, f32[1,512]{1,0:T(1,128)} %bitcast.1, s32[2,128]{1,0:T(2,128)} %crossing_hbm.1, s32[2,4,1024]{2,1,0:T(4,128)} %csend_hbm.1, s32[2,4,1024]{2,1,0:T(4,128)} %crecv_hbm.1, s32[2,4,8]{2,1,0:T(4,128)} %cfill_hbm.1, f32[128,256]{1,0:T(8,128)} %constant.4.clone.mats_hbm, ...), custom_call_target="tpu_custom_call" | custom-call | tf_op jit(solution)/shard_map/pallas_call | solution.py:427
  28.0 0.9 %copy.10 = f32[6,64,512]{2,1,0:T(8,128)} copy(f32[6,64,512]{2,1,0:T(8,128)S(1)} %shard_map.82) | data formatting | bytes 1572864
